TPU v7x, 32 devices: a whole 2x2x4 slice. The times are simulated.
32 devices in a mesh: parts: 2 (over y), seq: 4 (over x, core), tensor: 4 (over z).
Axes of the slice: x: 2, y: 2, z: 4, core: 2. Of those that a mesh axis runs over, the one named last changes fastest.
Arguments:
- token_ids: int32 [2048], P(('parts', 'seq')), parts along dimension 0, may hold values from 0 to 511
- embed: bfloat16 [512, 8192], P(None, 'tensor'), may hold values from -6 to 6
- norm_gain_vector: float32 [8192], P('tensor'), may hold values from 0.25 to 1.75
- base_proj: bfloat16 [3, 2048, 8192], P(None, ('parts', 'seq'), 'tensor'), parts along dimension 1, may hold values from -6 to 6
- adapter_down_matrices: bfloat16 [8192, 384], P('tensor'), may hold values from -0.0625 to 0.0625
- adapter_up_matrices: bfloat16 [3, 128, 8192], P(None, None, 'tensor'), may hold values from -0.5 to 0.5
- short_taps: float32 [3, 7, 8192], P(None, None, 'tensor'), may hold values from -2 to 2
- medium_taps: float32 [128, 8192], P(None, 'tensor'), may hold values from -0.5 to 0.5
- skip_gain: float32 [8192], P('tensor'), may hold values from 0.25 to 1.75
- mixer_cot: bfloat16 [2048, 8192], P(('parts', 'seq'), 'tensor'), parts along dimension 0, may hold values from -6 to 6
- bucket_ids: int32 [8192], P('tensor'), may hold values from 0 to 31
Outputs:
- features: float32 [4, 16, 384], P('parts'), parts along dimension 0
There are 2 independent parts, one for each index of `parts`. A program takes and returns all parts, laid end to end along the dimension named above; an argument that names none is the same for every part. Nothing has to cross between parts.
All inputs are finite; a program needn't handle non-finite values.
Results may differ from a plain program's by a relative error of at most 0.0069.
Values sent between devices are 32-bit elements; how exact they have to be, the bound alone decides.
A program may use at most 192 MiB of HBM per device.

v0:
```python
import jax
import jax.numpy as jnp
import numpy as np
from jax import lax
from jax.sharding import PartitionSpec as P

BUCKETS = 16
NORM_EPS = 1e-05
FEATURE_EPS = 1e-06
ADAPTER_SCALE = 1.5
RIM = 8
BF = jnp.bfloat16
F32 = jnp.float32


def from_behind(array, axis, by):
    count = lax.axis_size(axis)
    pairs = [(i, i + by) for i in range(count) if 0 <= i + by < count]
    return lax.ppermute(array, axis, pairs)


def spectrum_tables(rows, span):
    ext = rows + RIM + span
    half = -(-ext // 32) * 16
    period = 2 * half
    omega = 2.0 * np.pi * (np.arange(half) + 0.5) / period
    angle = omega[:, None] * np.arange(ext)[None, :]
    fwd = np.concatenate([np.cos(angle), -np.sin(angle)], axis=0)
    inv = fwd.T * (4.0 / period)
    return fwd, inv


def on_device(
    token_ids,
    embed,
    norm_gain_vector,
    base_proj,
    adapter_down_matrices,
    adapter_up_matrices,
    short_taps,
    medium_taps,
    skip_gain,
    mixer_cot,
    bucket_ids,
):
    rows = token_ids.shape[0]
    vocab = embed.shape[0]
    width = embed.shape[1]
    rank = adapter_up_matrices.shape[1]
    span = medium_taps.shape[0]
    taps = short_taps.shape[1]
    full = width * lax.axis_size("tensor")
    out_rows = rows + RIM

    ids = token_ids + 1
    ids_ext = jnp.concatenate(
        [from_behind(ids[rows - RIM :], "seq", 1), ids, from_behind(ids[:RIM], "seq", -1)]
    )
    base_ext = jnp.concatenate(
        [
            from_behind(base_proj[:, rows - RIM :].astype(F32), "seq", 1),
            base_proj.astype(F32),
            from_behind(base_proj[:, :RIM].astype(F32), "seq", -1),
        ],
        axis=1,
    )
    cot = mixer_cot.astype(F32)
    cot_ext = jnp.concatenate([cot, from_behind(cot[:RIM], "seq", -1)], axis=0)

    sketch = jnp.where(bucket_ids >= BUCKETS, -1.0, 1.0)[:, None] * (
        (bucket_ids % BUCKETS)[:, None] == jnp.arange(BUCKETS, dtype=jnp.int32)[None, :]
    )
    sketch = sketch.astype(BF)

    one_hot = (ids_ext[:, None] == 1 + jnp.arange(vocab, dtype=jnp.int32)[None, :]).astype(BF)
    inputs = jnp.dot(one_hot, embed, preferred_element_type=F32)
    squares = jnp.sum(inputs * inputs, axis=1, keepdims=True)
    gained = (inputs * norm_gain_vector).astype(BF)
    down = jnp.concatenate([adapter_down_matrices, sketch], axis=1)
    piece = jnp.dot(gained, down, preferred_element_type=F32)
    total = lax.psum(jnp.concatenate([piece, squares], axis=1), "tensor")
    scale = lax.rsqrt(total[:, -1:] / full + NORM_EPS)
    low = (total[:, : 3 * rank] * (scale * ADAPTER_SCALE)).astype(BF)
    token_sketch = (total[:, 3 * rank : -1] * scale)[RIM : RIM + rows]

    pre_mix = base_ext + jnp.einsum(
        "tsr,src->stc",
        low.reshape(-1, 3, rank),
        adapter_up_matrices,
        preferred_element_type=F32,
    )
    filtered = sum(
        short_taps[:, j][:, None, :] * pre_mix[:, RIM - j : RIM - j + out_rows]
        for j in range(taps)
    )
    key_value = filtered[1] * filtered[2]
    grad_mixed = cot_ext * filtered[0]
    kv_ext = jnp.concatenate(
        [from_behind(key_value[rows - span : rows], "seq", 1), key_value], axis=0
    )
    gm_ext = jnp.concatenate(
        [grad_mixed[:rows], from_behind(grad_mixed[: span + RIM], "seq", -1)], axis=0
    )

    fwd, inv = spectrum_tables(rows, span)
    half = fwd.shape[0] // 2
    fwd_t = jnp.asarray(fwd, BF)
    h = jnp.dot(fwd_t[:, :span], medium_taps.astype(BF), preferred_element_type=F32)
    x = jnp.dot(fwd_t, (kv_ext * 0.5).astype(BF), preferred_element_type=F32)
    g = jnp.dot(fwd_t, (gm_ext * 0.5).astype(BF), preferred_element_type=F32)
    hr, hi = h[:half], h[half:]
    xr, xi = x[:half], x[half:]
    gr, gi = g[:half], g[half:]
    y = jnp.concatenate([xr * hr - xi * hi, xr * hi + xi * hr], axis=0).astype(BF)
    z = jnp.concatenate([gr * hr + gi * hi, gi * hr - gr * hi], axis=0).astype(BF)
    mixed = (
        jnp.dot(jnp.asarray(inv[span : span + out_rows], BF), y, preferred_element_type=F32)
        + skip_gain * key_value
    )
    grad_kv = (
        jnp.dot(jnp.asarray(inv[:out_rows], BF), z, preferred_element_type=F32)
        + skip_gain * gm_ext[:out_rows]
    )
    streams = jnp.stack([cot_ext * mixed, grad_kv * filtered[2], grad_kv * filtered[1]])
    grad_pre = sum(
        short_taps[:, j][:, None, :] * streams[:, j : j + rows] for j in range(taps)
    ).astype(BF)

    wide = jnp.concatenate(
        [adapter_up_matrices, jnp.broadcast_to(sketch.T[None], (3, BUCKETS, width))], axis=1
    )
    prods = jnp.einsum("stc,skc->stk", grad_pre, wide, preferred_element_type=F32)
    sketch_in = ADAPTER_SCALE * jnp.einsum(
        "tk,str->ksr", token_sketch, prods[:, :, :rank], precision=lax.Precision.HIGHEST
    )
    sketch_out = jnp.einsum(
        "stk,tsr->ksr",
        prods[:, :, rank:],
        low[RIM : RIM + rows].reshape(rows, 3, rank).astype(F32),
        precision=lax.Precision.HIGHEST,
    )
    raw = jnp.stack([sketch_in, sketch_out]).reshape(2, BUCKETS, 3 * rank)
    raw = lax.psum(raw, ("seq", "tensor"))
    return raw * lax.rsqrt(jnp.mean(raw * raw) + FEATURE_EPS)


def solution(mesh):
    in_specs = (
        P(("parts", "seq")),
        P(None, "tensor"),
        P("tensor"),
        P(None, ("parts", "seq"), "tensor"),
        P("tensor", None),
        P(None, None, "tensor"),
        P(None, None, "tensor"),
        P(None, "tensor"),
        P("tensor"),
        P(("parts", "seq"), "tensor"),
        P("tensor"),
    )
    out_specs = P("parts", None, None)
    return jax.shard_map(
        on_device, mesh=mesh, in_specs=in_specs, out_specs=out_specs, check_vma=False
    )
```

profile of v0, /device:TPU:0, one launch (start us, length us, event | category | flops | bytes accessed | tf_op | source)
XLA Modules:
  0.0 207.1 jit_solution(11315392443431153149)
XLA Ops:
  6.5 0.8 broadcast_add_fusion
  7.4 2.3 %collective-permute-start = (s32[8]{0:T(128)S(1)}, s32[8]{0:T(128)S(1)}, u32[]{:S(2)}, u32[]{:S(2)}) collective-permute-start(s32[8]{0:T(128)S(1)} %get-tuple-element.20), channel_id=1, source_target_pairs={{0,4},{4,8},{8,12},{1,5},{5,9},{9,13},{2,6},{6,10},{10,14},{3,7},{... | collective-permute-start | bytes 104 | tf_op jit(solution)/shard_map/ppermute | solution.py:19
  9.8 1.3 collective-permute-start.1
  11.1 1.4 slice.205
  12.5 1.3 collective-permute-start.2
  13.8 1.7 slice_convert_fusion.1
  15.5 5.8 %collective-permute-start.3 = (f32[3,8,2048]{2,1,0:T(8,128)}, f32[3,8,2048]{2,1,0:T(8,128)S(1)}, u32[]{:S(2)}, u32[]{:S(2)}) collective-permute-start(f32[3,8,2048]{2,1,0:T(8,128)} %get-tuple-element.11), channel_id=1, source_target_pairs={{0,4},{4,8},{8,12},{1,5},{5,9},{9,13},{2,6},{6,10},{10,14},{3,7},{... | collective-permute-start | bytes 589832 | tf_op jit(solution)/shard_map/ppermute | solution.py:19
  21.2 1.3 collective-permute-start.4
  24.0 2.7 %fusion.71 = (f32[3,1,2048]{2,1,0:T(1,128)}, f32[3,1,2048]{2,1,0:T(1,128)S(1)}, f32[3,1,2048]{2,1,0:T(1,128)S(1)}, f32[3,1,2048]{2,1,0:T(1,128)S(1)}, f32[3,1,20...) fusion(f32[3,7,2048]{2,1,0:T(8,128)} %param.20), kind=kLoop, calls=%fused_computation.129 | loop fusion | bytes 344064 | tf_op jit(solution)/shard_map/slice | solution.py:126
  27.6 0.9 multiply_reduce_fusion
  29.5 0.9 pad_maximum_fusion.3
  31.3 6.1 %convert_element_type.49 = f32[3,256,2048]{2,1,0:T(8,128)} convert(bf16[3,256,2048]{2,1,0:T(8,128)(2,1)} %param.17) | non-fusion elementwise | flops 1572864 | bytes 9437184 | tf_op jit(solution)/shard_map/convert_element_type | solution.py:62
  37.5 35.6 %all-reduce.2.cloned.1.call-done = f32[272,401]{1,0:T(8,128)} async-done(((f32[272,401]{1,0:T(8,128)}), f32[272,401]{1,0:T(8,128)}) %all-reduce.2.cloned.1.call-update) | async-done | bytes 436304 | tf_op jit(solution)/shard_map/psum | solution.py:81
  73.1 1.2 fusion.61
  74.3 4.4 %maximum_add_fusion = f32[3,272,2048]{2,1,0:T(8,128)S(1)} fusion(f32[3,8,2048]{2,1,0:T(8,128)} %collective-permute-done.4, f32[3,256,2048]{2,1,0:T(8,128)} %convert_element_type.49, f32[3,8,2048]{2,1,0:T(8,128)S(1)} %collective-permute-done.3, bf16[3,128,2048]{2,1,0:T(8,128)(2,1)} %param.19, f32[272]{0:T(512)S(1)} %get-tuple-element.6, ...), kind=kOutput, calls=%fused_computation | convolution fusion | flops 433041408 | bytes 15361088 | tf_op jit(solution)/shard_map/tsr,src->stc/dot_general | solution.py:86
  78.8 5.3 %fusion = f32[3,264,2048]{2,1,0:T(8,128)S(1)} fusion(f32[3,272,2048]{2,1,0:T(8,128)S(1)} %maximum_add_fusion, f32[3,2048]{1,0:T(4,128)S(1)} %copy-done.25, f32[3,2048]{1,0:T(4,128)S(1)} %copy-done.27, f32[3,2048]{1,0:T(4,128)S(1)} %get-tuple-element.26, f32[3,2048]{1,0:T(4,128)S(1)} %get-tuple-element.27, f32[3,2048]{1,0:T(4,128)S(1)} %get-tuple-element.28, ...), kind=kLoop, calls=%fused_computation.2 | loop fusion | flops 21086208 | bytes 52076544 | tf_op jit(solution)/shard_map/add | solution.py:92
  84.2 0.8 fusion.31
  85.0 1.9 copy-done.2
  86.9 1.1 slice.216
  88.6 2.3 %collective-permute-start.5 = (f32[128,2048]{1,0:T(8,128)}, f32[128,2048]{1,0:T(8,128)}, u32[]{:S(2)}, u32[]{:S(2)}) collective-permute-start(f32[128,2048]{1,0:T(8,128)} %slice.216), channel_id=1, source_target_pairs={{0,4},{4,8},{8,12},{1,5},{5,9},{9,13},{2,6},{6,10},{10,14},{3,7},{... | collective-permute-start | bytes 3145736 | tf_op jit(solution)/shard_map/ppermute | solution.py:19
  91.6 1.1 slice.223
  92.7 1.6 slice.222
  95.1 1.7 copy.24
  96.9 1.5 collective-permute-start.6
  98.3 3.1 %fusion.35 = f32[416,2048]{1,0:T(8,128)S(1)} fusion(bf16[416,392]{1,0:T(8,128)(2,1)} %constant.47.clone, f32[264,2048]{1,0:T(8,128)} %copy-done.3, f32[128,2048]{1,0:T(8,128)} %collective-permute-done.5), kind=kOutput, calls=%fused_computation.68 | convolution fusion | flops 670351360 | bytes 6945280 | tf_op jit(solution)/shard_map/dot_general | solution.py:109
  102.2 0.9 copy-done.4
  103.7 0.9 fusion.22
  105.3 1.1 fusion.37
  107.3 2.8 %multiply_bitcast_fusion.1 = (f32[1,264,2048]{2,1,0:T(8,128)S(1)}, f32[1,264,2048]{2,1,0:T(8,128)S(1)}) fusion(f32[3,264,2048]{2,1,0:T(8,128)} %copy-done.2, f32[136,2048]{1,0:T(8,128)S(1)} %collective-permute-done.6, f32[256,2048]{1,0:T(8,128)S(1)} %copy-done.7, f32[2048]{0:T(1024)S(1)} %copy-done.35, f32[2048,264]{0,1:T(8,128)S(1)} %fusion.43, ...), kind=kOutput, calls=%fused_computation.55 | convolution fusion | flops 229867520 | bytes 20958464 | tf_op jit(solution)/shard_map/dot_general | solution.py:121
  110.2 3.2 %pad_maximum_fusion = f32[3,264,2048]{2,1,0:T(8,128)} fusion(f32[1,264,2048]{2,1,0:T(8,128)S(1)} %get-tuple-element.8, f32[1,264,2048]{2,1,0:T(8,128)S(1)} %get-tuple-element.7, f32[1,264,2048]{2,1,0:T(8,128)S(1)} %fusion.22), kind=kLoop, calls=%fused_computation.14 | loop fusion | flops 3244032 | bytes 12976128 | tf_op jit(solution)/shard_map/stack | solution.py:124
  113.5 18.6 %fusion.16 = f32[3,256,144]{1,2,0:T(8,128)S(1)} fusion(f32[3,264,2048]{2,1,0:T(8,128)} %pad_maximum_fusion, f32[3,2048]{1,0:T(4,128)S(1)} %copy-done.26, f32[3,2048]{1,0:T(4,128)S(1)} %copy-done.28, f32[3,2048]{1,0:T(4,128)S(1)} %copy-done.18, f32[3,2048]{1,0:T(4,128)S(1)} %copy-done.20, f32[3,2048]{1,0:T(4,128)S(1)} %copy-done.22, ...), kind=kOutput, calls=%fused_computation.36 | convolution fusion | flops 478543872 | bytes 46424064 | tf_op jit(solution)/shard_map/stc,skc->stk/dot_general | solution.py:132
  133.1 65.2 %psum.15 = f32[2,16,384]{2,1,0:T(8,128)S(1)} all-reduce(f32[2,16,384]{2,1,0:T(8,128)S(1)} %pad_maximum_fusion.4), channel_id=1, replica_groups=mesh['parts'=2,'seq'=4,'tensor'=4] {'seq','tensor'}, use_global_device_ids=true, to_apply=%region_2.3 | all-reduce | flops 12288 | bytes 98304 | tf_op jit(solution)/shard_map/psum | solution.py:143
  (115 shorter events, 11.5 us)
Async XLA Ops:
  6.5 21.1 %copy-start = (bf16[512,2048]{1,0:T(8,128)(2,1)S(1)}, bf16[512,2048]{1,0:T(8,128)(2,1)}, u32[]{:S(2)}) copy-start(bf16[512,2048]{1,0:T(8,128)(2,1)} %param.15) | copy-start | bytes 6291460
  6.5 66.6 %all-reduce.2.cloned.1.call-start = ((), (), s32[]{:S(2)}) async-start(), calls=%async_computation | async-start | bytes 1114112 | tf_op jit(solution)/shard_map/psum | solution.py:81
  7.4 20.1 %collective-permute-start = (s32[8]{0:T(128)S(1)}, s32[8]{0:T(128)S(1)}, u32[]{:S(2)}, u32[]{:S(2)}) collective-permute-start(s32[8]{0:T(128)S(1)} %get-tuple-element.20), channel_id=1, source_target_pairs={{0,4},{4,8},{8,12},{1,5},{5,9},{9,13},{2,6},{6,10},{10,14},{3,7},{... | collective-permute-start | bytes 104 | tf_op jit(solution)/shard_map/ppermute | solution.py:19
  9.8 17.7 %collective-permute-start.1 = (s32[8]{0:T(128)S(1)}, s32[8]{0:T(128)S(1)}, u32[]{:S(2)}, u32[]{:S(2)}) collective-permute-start(s32[8]{0:T(128)S(1)} %get-tuple-element.21), channel_id=1, source_target_pairs={{4,0},{8,4},{12,8},{5,1},{9,5},{13,9},{6,2},{10,6},{14,10},{7,3},{... | collective-permute-start | bytes 104 | tf_op jit(solution)/shard_map/ppermute | solution.py:19
  12.5 71.7 %collective-permute-start.2 = (f32[8,2048]{1,0:T(8,128)}, f32[8,2048]{1,0:T(8,128)S(1)}, u32[]{:S(2)}, u32[]{:S(2)}) collective-permute-start(f32[8,2048]{1,0:T(8,128)} %slice.205), channel_id=1, source_target_pairs={{4,0},{8,4},{12,8},{5,1},{9,5},{13,9},{6,2},{10,6},{14,10},{7,3},{... | collective-permute-start | bytes 196616 | tf_op jit(solution)/shard_map/ppermute | solution.py:19
  15.5 58.8 %collective-permute-start.3 = (f32[3,8,2048]{2,1,0:T(8,128)}, f32[3,8,2048]{2,1,0:T(8,128)S(1)}, u32[]{:S(2)}, u32[]{:S(2)}) collective-permute-start(f32[3,8,2048]{2,1,0:T(8,128)} %get-tuple-element.11), channel_id=1, source_target_pairs={{0,4},{4,8},{8,12},{1,5},{5,9},{9,13},{2,6},{6,10},{10,14},{3,7},{... | collective-permute-start | bytes 589832 | tf_op jit(solution)/shard_map/ppermute | solution.py:19
  21.2 53.0 %collective-permute-start.4 = (f32[3,8,2048]{2,1,0:T(8,128)}, f32[3,8,2048]{2,1,0:T(8,128)}, u32[]{:S(2)}, u32[]{:S(2)}) collective-permute-start(f32[3,8,2048]{2,1,0:T(8,128)} %get-tuple-element.12), channel_id=1, source_target_pairs={{4,0},{8,4},{12,8},{5,1},{9,5},{13,9},{6,2},{10,6},{14,10},{7,3},{... | collective-permute-start | bytes 589832 | tf_op jit(solution)/shard_map/ppermute | solution.py:19
  26.7 52.0 %copy-start.17 = (f32[3,2048]{1,0:T(4,128)}, f32[3,2048]{1,0:T(4,128)S(1)}, u32[]{:S(2)}) copy-start(f32[3,2048]{1,0:T(4,128)S(1)} %get-tuple-element.26) | copy-start | bytes 73732
  26.7 52.0 %copy-start.19 = (f32[3,2048]{1,0:T(4,128)}, f32[3,2048]{1,0:T(4,128)S(1)}, u32[]{:S(2)}) copy-start(f32[3,2048]{1,0:T(4,128)S(1)} %get-tuple-element.27) | copy-start | bytes 73732
  26.8 52.0 %copy-start.21 = (f32[3,2048]{1,0:T(4,128)}, f32[3,2048]{1,0:T(4,128)S(1)}, u32[]{:S(2)}) copy-start(f32[3,2048]{1,0:T(4,128)S(1)} %get-tuple-element.28) | copy-start | bytes 73732
  26.8 52.0 %copy-start.23 = (f32[3,2048]{1,0:T(4,128)}, f32[3,2048]{1,0:T(4,128)S(1)}, u32[]{:S(2)}) copy-start(f32[3,2048]{1,0:T(4,128)S(1)} %get-tuple-element.29) | copy-start | bytes 73732
  31.3 52.9 %copy-start.5 = (f32[256,2048]{1,0:T(8,128)}, f32[256,2048]{1,0:T(8,128)S(1)}, u32[]{:S(2)}) copy-start(f32[256,2048]{1,0:T(8,128)S(1)} %convert_element_type.47) | copy-start | bytes 6291460
  31.3 6.2 %copy-start.32 = (f32[3,1,2048]{2,1,0:T(1,128)S(1)}, f32[3,1,2048]{2,1,0:T(1,128)}, u32[]{:S(2)}) copy-start(f32[3,1,2048]{2,1,0:T(1,128)} %get-tuple-element.13) | copy-start | bytes 73732
  37.5 41.3 %copy-start.29 = (f32[3,1,2048]{2,0,1:T(4,128)}, f32[3,1,2048]{2,0,1:T(4,128)S(1)}, u32[]{:S(2)}) copy-start(f32[3,1,2048]{2,0,1:T(4,128)S(1)} %copy.50) | copy-start | bytes 73732
  74.3 4.5 %copy-start.25 = (f32[3,2048]{1,0:T(4,128)S(1)}, f32[3,2048]{1,0:T(4,128)}, u32[]{:S(2)}) copy-start(f32[3,2048]{1,0:T(4,128)} %get-tuple-element.24) | copy-start | bytes 73732
  74.3 4.5 %copy-start.27 = (f32[3,2048]{1,0:T(4,128)S(1)}, f32[3,2048]{1,0:T(4,128)}, u32[]{:S(2)}) copy-start(f32[3,2048]{1,0:T(4,128)} %get-tuple-element.25) | copy-start | bytes 73732
  84.1 2.7 %copy-start.2 = (f32[3,264,2048]{2,1,0:T(8,128)}, f32[3,264,2048]{2,1,0:T(8,128)S(1)}, u32[]{:S(2)}) copy-start(f32[3,264,2048]{2,1,0:T(8,128)S(1)} %fusion) | copy-start | bytes 19464196
  84.1 6.8 %copy-start.11 = (f32[128,2048]{1,0:T(8,128)S(1)}, f32[128,2048]{1,0:T(8,128)}, u32[]{:S(2)}) copy-start(f32[128,2048]{1,0:T(8,128)} %param.21) | copy-start | bytes 3145732
  84.2 6.8 %copy-start.31 = (bf16[416,128]{1,0:T(8,128)(2,1)S(1)}, bf16[416,128]{1,0:T(8,128)(2,1)}, u32[]{:S(2)}) copy-start(bf16[416,128]{1,0:T(8,128)(2,1)} %constant.50) | copy-start | bytes 319492
  88.6 9.7 %collective-permute-start.5 = (f32[128,2048]{1,0:T(8,128)}, f32[128,2048]{1,0:T(8,128)}, u32[]{:S(2)}, u32[]{:S(2)}) collective-permute-start(f32[128,2048]{1,0:T(8,128)} %slice.216), channel_id=1, source_target_pairs={{0,4},{4,8},{8,12},{1,5},{5,9},{9,13},{2,6},{6,10},{10,14},{3,7},{... | collective-permute-start | bytes 3145736 | tf_op jit(solution)/shard_map/ppermute | solution.py:19
  96.9 7.8 %collective-permute-start.6 = (f32[136,2048]{1,0:T(8,128)}, f32[136,2048]{1,0:T(8,128)S(1)}, u32[]{:S(2)}, u32[]{:S(2)}) collective-permute-start(f32[136,2048]{1,0:T(8,128)} %slice.223), channel_id=1, source_target_pairs={{4,0},{8,4},{12,8},{5,1},{9,5},{13,9},{6,2},{10,6},{14,10},{7,3},{... | collective-permute-start | bytes 3342344 | tf_op jit(solution)/shard_map/ppermute | solution.py:19
  98.3 3.1 %copy-start.14 = (bf16[264,208]{1,0:T(8,128)(2,1)S(1)}, bf16[264,208]{1,0:T(8,128)(2,1)}, u32[]{:S(2)}) copy-start(bf16[264,208]{1,0:T(8,128)(2,1)} %constant.51) | copy-start | bytes 329476
  110.1 3.3 %copy-start.18 = (f32[3,2048]{1,0:T(4,128)S(1)}, f32[3,2048]{1,0:T(4,128)}, u32[]{:S(2)}) copy-start(f32[3,2048]{1,0:T(4,128)} %copy-done.17) | copy-start | bytes 73732
  110.1 3.3 %copy-start.20 = (f32[3,2048]{1,0:T(4,128)S(1)}, f32[3,2048]{1,0:T(4,128)}, u32[]{:S(2)}) copy-start(f32[3,2048]{1,0:T(4,128)} %copy-done.19) | copy-start | bytes 73732
  110.1 3.3 %copy-start.22 = (f32[3,2048]{1,0:T(4,128)S(1)}, f32[3,2048]{1,0:T(4,128)}, u32[]{:S(2)}) copy-start(f32[3,2048]{1,0:T(4,128)} %copy-done.21) | copy-start | bytes 73732
  110.1 3.3 %copy-start.24 = (f32[3,2048]{1,0:T(4,128)S(1)}, f32[3,2048]{1,0:T(4,128)}, u32[]{:S(2)}) copy-start(f32[3,2048]{1,0:T(4,128)} %copy-done.23) | copy-start | bytes 73732
  110.1 3.3 %copy-start.26 = (f32[3,2048]{1,0:T(4,128)S(1)}, f32[3,2048]{1,0:T(4,128)}, u32[]{:S(2)}) copy-start(f32[3,2048]{1,0:T(4,128)} %get-tuple-element.24) | copy-start | bytes 73732
  110.1 3.3 %copy-start.28 = (f32[3,2048]{1,0:T(4,128)S(1)}, f32[3,2048]{1,0:T(4,128)}, u32[]{:S(2)}) copy-start(f32[3,2048]{1,0:T(4,128)} %get-tuple-element.25) | copy-start | bytes 73732
  110.1 3.3 %copy-start.30 = (f32[3,1,2048]{2,0,1:T(4,128)S(1)}, f32[3,1,2048]{2,0,1:T(4,128)}, u32[]{:S(2)}) copy-start(f32[3,1,2048]{2,0,1:T(4,128)} %copy-done.29) | copy-start | bytes 73732
  113.4 18.7 %copy-start.12 = (bf16[256,384]{0,1:T(8,128)(2,1)S(1)}, bf16[256,384]{0,1:T(8,128)(2,1)}, u32[]{:S(2)}) copy-start(bf16[256,384]{0,1:T(8,128)(2,1)} %copy.24) | copy-start | bytes 589828
  113.4 18.9 %slice-start = ((f32[272,401]{1,0:T(8,128)}), f32[272,16]{1,0:T(8,128)S(1)}, s32[]{:S(2)}) async-start(f32[272,401]{1,0:T(8,128)} %all-reduce.2.cloned.1.call-done), calls=%async_computation.1 | async-start | bytes 278528 | tf_op jit(solution)/shard_map/slice | solution.py:84
  113.4 86.8 %copy-start.1 = (bf16[512,2048]{1,0:T(8,128)(2,1)S(1)}, bf16[512,2048]{1,0:T(8,128)(2,1)}, u32[]{:S(2)}) copy-start(bf16[512,2048]{1,0:T(8,128)(2,1)} %param.15) | copy-start | bytes 6291460
  (15 other events, 28.4 us)
Sparse Core Ops, SparseCore 0:
  30.5 42.5 all-reduce.1
where the time goes:
time: 211 us; the launch traced here: 207 us
  blocking collectives  65.2 us (31%)
  waiting for transfers between devices  35.6 us (17%)
  matrix products  35.3 us (17%)
  other arithmetic  23.9 us (11%)
  local copies, waits for them, and re-layouts  16.5 us (8%)
  starting transfers between devices  15.8 us (7%)
  between operations  14.8 us (7%)
    psum x1, blocking collectives, on_device(): raw = lax.psum(raw, ('seq', 'tensor'))  65.2 us
    psum x1, waiting for transfers between devices, on_device(): total = lax.psum(jnp.concatenate([piece, squares], axis=1), 'tensor')  35.6 us
    dot_general x1, matrix products, on_device(): jnp.einsum('stc,skc->stk', grad_pre, wide, preferred_element_type=F32)  18.6 us
    ppermute x7, starting transfers between devices, from_behind(): return lax.ppermute(array, axis, pairs)  15.8 us
    convert_element_type x1, other arithmetic, on_device(): base_proj.astype(F32)  6.15 us
    unnamed x80, local copies, waits for them, and re-layouts  5.83 us
    add x1, other arithmetic, on_device(): sum((short_taps[:, j][:, None, :] * pre_mix[:, RIM - j:RIM - j + out_rows...  5.34 us
    dot_general x1, matrix products, on_device(): jnp.einsum('tsr,src->stc', low.reshape(-1, 3, rank), adapter_up_matrices,...  4.39 us
  transfers between devices with their start and end apart: 8, of which 1 were waited for; matrix products, arithmetic and copies ran while one was open for 19% of the time, Pallas kernels for 0%

commit v1 on v0

v1 whole, which is shorter than its diff:
```python
import functools

import jax
import jax.numpy as jnp
import numpy as np
from jax import lax
from jax.experimental import pallas as pl
from jax.experimental.pallas import tpu as pltpu
from jax.sharding import PartitionSpec as P

BUCKETS = 16
NORM_EPS = 1e-05
FEATURE_EPS = 1e-06
ADAPTER_SCALE = 1.5
RIM = 8
CHUNK = 256
BF = jnp.bfloat16
F32 = jnp.float32
HIGHEST = lax.Precision.HIGHEST
MESH = pl.DeviceIdType.MESH


def ceil_to(count, step):
    return -(-count // step) * step


def spectrum_tables(rows, span):
    ext = ceil_to(rows + RIM + span, 16)
    half = ceil_to(ext, 32) // 2
    period = 2 * half
    omega = 2.0 * np.pi * (np.arange(half) + 0.5) / period
    angle = omega[:, None] * np.arange(ext + 16)[None, :]
    fwd = np.concatenate([np.cos(angle), -np.sin(angle)], axis=0)
    inv = fwd.T * (2.0 / period)
    out_rows = ceil_to(rows + RIM, 16)
    return fwd[:, :ext], inv[span : span + out_rows], inv[:out_rows]


def nn(a, b):
    return jnp.dot(a, b, preferred_element_type=F32)


def nt(a, b):
    return lax.dot_general(a, b, (((1,), (1,)), ((), ())), preferred_element_type=F32)


def tn(a, b):
    return lax.dot_general(
        a, b, (((0,), (0,)), ((), ())), precision=HIGHEST, preferred_element_type=F32
    )


def kernel(
    ns,
    nz,
    ids_ref,
    embed_ref,
    gain_ref,
    base_hbm,
    down_ref,
    up_hbm,
    short_ref,
    medium_ref,
    skip_ref,
    cot_hbm,
    bucket_ref,
    fwd_ref,
    inv1_ref,
    inv2_ref,
    out_ref,
    ids_ext,
    one_hot,
    base,
    up,
    cot,
    sketch,
    to_prev,
    to_next,
    from_next,
    from_prev,
    acc,
    rs,
    low,
    psk,
    spec,
    kv,
    gm,
    fk,
    fv,
    prods,
    part_z,
    part_s,
    load_sem,
    rim_send,
    rim_recv,
    rs_send,
    rs_recv,
    ag_send,
    ag_recv,
    kv_send,
    kv_recv,
    gm_send,
    gm_recv,
    fz_send,
    fz_recv,
    fs_send,
    fs_recv,
):
    rows = ids_ref.shape[0]
    vocab, width = embed_ref.shape
    rank = up_hbm.shape[1]
    span = medium_ref.shape[0]
    taps = short_ref.shape[1]
    padded = acc.shape[0]
    own_rows = padded // nz
    out_rows = rows + RIM
    all_rows = rows + 2 * RIM
    ext = kv.shape[1]
    half = fwd_ref.shape[0] // 2
    chunks = width // CHUNK
    wide = 3 * rank
    s_me = lax.axis_index("seq")
    z_me = lax.axis_index("tensor")
    has_prev = s_me > 0
    has_next = s_me < ns - 1
    prev = {"seq": lax.rem(s_me + ns - 1, ns)}
    succ = {"seq": lax.rem(s_me + 1, ns)}

    loads = [
        pltpu.make_async_copy(src, dst, load_sem.at[i])
        for i, (src, dst) in enumerate([(base_hbm, base), (up_hbm, up), (cot_hbm, cot)])
    ]
    for load in loads:
        load.start()

    barrier = pltpu.get_barrier_semaphore()
    for d in range(1, ns):
        pl.semaphore_signal(
            barrier, inc=1, device_id={"seq": lax.rem(s_me + d, ns)}, device_id_type=MESH
        )
    for d in range(1, nz):
        pl.semaphore_signal(
            barrier, inc=1, device_id={"tensor": lax.rem(z_me + d, nz)}, device_id_type=MESH
        )
    pl.semaphore_wait(barrier, ns + nz - 2)

    def remote(src, dst, send, recv, device):
        return pltpu.make_async_remote_copy(
            src_ref=src,
            dst_ref=dst,
            send_sem=send,
            recv_sem=recv,
            device_id=device,
            device_id_type=MESH,
        )

    ids_to_next = remote(
        ids_ref.at[rows - RIM : rows], ids_ext.at[0:RIM], rim_send.at[0], rim_recv.at[0], succ
    )
    ids_to_prev = remote(
        ids_ref.at[0:RIM],
        ids_ext.at[RIM + rows : all_rows],
        rim_send.at[1],
        rim_recv.at[1],
        prev,
    )
    rim_to_next = remote(to_next, from_prev, rim_send.at[2], rim_recv.at[2], succ)
    rim_to_prev = remote(to_prev, from_next, rim_send.at[3], rim_recv.at[3], prev)

    @pl.when(has_next)
    def _():
        ids_to_next.start()

    @pl.when(has_prev)
    def _():
        ids_to_prev.start()

    @pl.when(jnp.logical_not(has_prev))
    def _():
        ids_ext[0:RIM] = jnp.zeros((RIM, 128), jnp.int32)
        from_prev[...] = jnp.zeros_like(from_prev)
        for k in range(chunks):
            kv[k, 0:span] = jnp.zeros((span, CHUNK), F32)

    @pl.when(jnp.logical_not(has_next))
    def _():
        ids_ext[RIM + rows : all_rows] = jnp.zeros((RIM, 128), jnp.int32)
        from_next[...] = jnp.zeros_like(from_next)
        for k in range(chunks):
            gm[k, rows : rows + span + RIM] = jnp.zeros((span + RIM, CHUNK), F32)

    tail = ext - (out_rows + span)
    if tail:
        for k in range(chunks):
            kv[k, ext - tail : ext] = jnp.zeros((tail, CHUNK), F32)
            gm[k, ext - tail : ext] = jnp.zeros((tail, CHUNK), F32)
    if padded > all_rows:
        ids_ext[all_rows:padded] = jnp.zeros((padded - all_rows, 128), jnp.int32)
    ids_ext[RIM : RIM + rows] = ids_ref[...]
    bucket = bucket_ref[...]
    hit = lax.broadcasted_iota(jnp.int32, (BUCKETS, width), 0) == jnp.bitwise_and(
        bucket, BUCKETS - 1
    )
    sign = jnp.where(bucket >= BUCKETS, -1.0, 1.0).astype(F32)
    sketch[...] = jnp.where(hit, sign, 0.0).astype(BF)
    acc[...] = jnp.zeros_like(acc)
    prods[...] = jnp.zeros_like(prods)

    loads[0].wait()
    loads[2].wait()
    for s in range(3):
        to_prev[s] = base[s, 0 : 2 * RIM].astype(F32)[:RIM]
        to_next[s] = base[s, rows - 2 * RIM : rows].astype(F32)[RIM:]
    to_prev[3] = cot[0 : 2 * RIM].astype(F32)[:RIM]

    @pl.when(has_next)
    def _():
        rim_to_next.start()

    @pl.when(has_prev)
    def _():
        rim_to_prev.start()

    @pl.when(has_prev)
    def _():
        ids_to_next.wait_recv()

    @pl.when(has_next)
    def _():
        ids_to_prev.wait_recv()

    ids = jnp.concatenate([ids_ext[...]] * (vocab // 128), axis=1)
    one_hot[...] = jnp.where(
        ids == lax.broadcasted_iota(jnp.int32, (padded, vocab), 1) + 1, 1.0, 0.0
    ).astype(BF)

    def at(k):
        return pl.ds(pl.multiple_of(k * CHUNK, CHUNK), CHUNK)

    def front(k, carry):
        cols = at(k)
        x = nn(one_hot[...], embed_ref[:, cols])
        squares = jnp.sum(x * x, axis=1, keepdims=True)
        gained = x * gain_ref[:, cols]
        high = gained.astype(BF)
        rest = (gained - high.astype(F32)).astype(BF)
        weights = down_ref[cols, :]
        acc[:, :wide] += nn(high, weights) + nn(rest, weights)
        table = sketch[:, cols]
        acc[:, wide : wide + BUCKETS] += nt(high, table) + nt(rest, table)
        acc[:, wide + BUCKETS : wide + BUCKETS + 1] += squares
        return carry

    lax.fori_loop(0, chunks, front, 0)

    def rows_of(z):
        return pl.ds(pl.multiple_of(z * own_rows, 8), own_rows)

    mine = rows_of(z_me)
    scatters = []
    for d in range(1, nz):
        z_to = lax.rem(z_me + d, nz)
        scatters.append(
            remote(
                acc.at[rows_of(z_to)],
                rs.at[d - 1],
                rs_send.at[d - 1],
                rs_recv.at[d - 1],
                {"tensor": z_to},
            )
        )
    for copy in scatters:
        copy.start()

    def filter_spectrum(k, carry):
        spec[k] = nn(fwd_ref[:, :span], medium_ref[:, at(k)].astype(BF))
        return carry

    lax.fori_loop(0, chunks, filter_spectrum, 0)

    total = acc[mine, :]
    for d in range(1, nz):
        scatters[d - 1].wait_recv()
        total = total + rs[d - 1]
    scale = lax.rsqrt(
        total[:, wide + BUCKETS : wide + BUCKETS + 1] / (width * nz) + NORM_EPS
    )
    low[mine, :] = (total[:, :wide] * (scale * ADAPTER_SCALE)).astype(BF).astype(F32)
    psk[mine, :] = total[:, wide:] * scale
    gathers = []
    for d in range(1, nz):
        peer = {"tensor": lax.rem(z_me + d, nz)}
        gathers.append(
            remote(
                low.at[mine], low.at[mine], ag_send.at[0, d - 1], ag_recv.at[0, d - 1], peer
            )
        )
    for d in range(1, nz):
        peer = {"tensor": lax.rem(z_me + d, nz)}
        gathers.append(
            remote(
                psk.at[mine], psk.at[mine], ag_send.at[1, d - 1], ag_recv.at[1, d - 1], peer
            )
        )
    for copy in gathers:
        copy.start()

    loads[1].wait()

    @pl.when(has_prev)
    def _():
        rim_to_next.wait_recv()

    @pl.when(has_next)
    def _():
        rim_to_prev.wait_recv()

    for copy in gathers[: nz - 1]:
        copy.wait_recv()

    def kv_copy(k):
        return remote(
            kv.at[k, rows : rows + span], kv.at[k, 0:span], kv_send.at[k], kv_recv.at[k], succ
        )

    def gm_copy(k):
        return remote(
            gm.at[k, 0 : span + RIM],
            gm.at[k, rows : rows + span + RIM],
            gm_send.at[k],
            gm_recv.at[k],
            prev,
        )

    def streams_in(k, carry):
        cols = at(k)
        filtered = []
        for s in range(3):
            pre = jnp.concatenate(
                [from_prev[s, :, cols], base[s, :, cols].astype(F32), from_next[s, :, cols]],
                axis=0,
            ) + nn(low[0:all_rows, s * rank : (s + 1) * rank].astype(BF), up[s, :, cols])
            coeff = short_ref[s, :, cols]
            running = coeff[0:1] * pre[RIM : RIM + out_rows]
            for j in range(1, taps):
                running = running + coeff[j : j + 1] * pre[RIM - j : RIM - j + out_rows]
            filtered.append(running)
        fk[k] = filtered[1]
        fv[k] = filtered[2]
        kv[k, span : span + out_rows] = filtered[1] * filtered[2]
        gm[k, 0:rows] = cot[:, cols].astype(F32) * filtered[0][0:rows]

        @pl.when(has_next)
        def _():
            kv_copy(k).start()

        @pl.when(has_prev)
        def _():
            gm_copy(k).start()

        return carry

    lax.fori_loop(0, chunks, streams_in, 0)

    def streams_back(k, carry):
        cols = at(k)

        @pl.when(has_prev)
        def _():
            kv_copy(k).wait_recv()

        @pl.when(has_next)
        def _():
            gm_copy(k).wait_recv()

        hr, hi = spec[k, 0:half], spec[k, half:]
        x = nn(fwd_ref[...], kv[k].astype(BF))
        xr, xi = x[:half], x[half:]
        y = jnp.concatenate([xr * hr - xi * hi, xr * hi + xi * hr], axis=0).astype(BF)
        skip = skip_ref[:, cols]
        mixed = nn(inv1_ref[...], y)[:out_rows] + skip * kv[k, span : span + out_rows]
        g = nn(fwd_ref[...], gm[k].astype(BF))
        gr, gi = g[:half], g[half:]
        w = jnp.concatenate([gr * hr + gi * hi, gi * hr - gr * hi], axis=0).astype(BF)
        grad_kv = nn(inv2_ref[...], w)[:out_rows] + skip * gm[k, 0:out_rows]
        cot_ext = jnp.concatenate([cot[:, cols].astype(F32), from_next[3, :, cols]], axis=0)
        table = sketch[:, cols]
        for s in range(3):
            if s == 0:
                stream = cot_ext * mixed
            elif s == 1:
                stream = grad_kv * fv[k]
            else:
                stream = grad_kv * fk[k]
            coeff = short_ref[s, :, cols]
            running = coeff[0:1] * stream[0:rows]
            for j in range(1, taps):
                running = running + coeff[j : j + 1] * stream[j : j + rows]
            joined = jnp.concatenate([up[s, :, cols], table], axis=0)
            prods[s] += nt(running.astype(BF), joined)
        return carry

    lax.fori_loop(0, chunks, streams_back, 0)

    for copy in gathers[nz - 1 :]:
        copy.wait_recv()
    token_sketch = psk[RIM : RIM + rows, 0:BUCKETS]
    for s in range(3):
        block = slice(s * rank, (s + 1) * rank)
        part_z[z_me, 0:BUCKETS, block] = ADAPTER_SCALE * tn(token_sketch, prods[s, :, 0:rank])
        part_z[z_me, BUCKETS : 2 * BUCKETS, block] = tn(
            prods[s, :, rank:], low[RIM : RIM + rows, block]
        )

    def share(buffer, me, count, axis, send, recv):
        copies = [
            remote(
                buffer.at[me],
                buffer.at[me],
                send.at[d - 1],
                recv.at[d - 1],
                {axis: lax.rem(me + d, count)},
            )
            for d in range(1, count)
        ]
        for copy in copies:
            copy.start()
        for copy in copies:
            copy.wait_recv()
        total = buffer[0]
        for i in range(1, count):
            total = total + buffer[i]
        return total, copies

    total, sent_z = share(part_z, z_me, nz, "tensor", fz_send, fz_recv)
    part_s[s_me] = total
    raw, sent_s = share(part_s, s_me, ns, "seq", fs_send, fs_recv)
    mean = jnp.sum(raw * raw) / (2 * BUCKETS * wide)
    features = raw * lax.rsqrt(jnp.full((1, wide), FEATURE_EPS, F32) + mean)
    out_ref[0] = features[:BUCKETS]
    out_ref[1] = features[BUCKETS:]

    for copy in scatters + gathers + sent_z + sent_s:
        copy.wait_send()

    @pl.when(has_next)
    def _():
        ids_to_next.wait_send()
        rim_to_next.wait_send()

        def drain(k, carry):
            kv_copy(k).wait_send()
            return carry

        lax.fori_loop(0, chunks, drain, 0)

    @pl.when(has_prev)
    def _():
        ids_to_prev.wait_send()
        rim_to_prev.wait_send()

        def drain(k, carry):
            gm_copy(k).wait_send()
            return carry

        lax.fori_loop(0, chunks, drain, 0)


def on_device(
    ns,
    nz,
    token_ids,
    embed,
    norm_gain_vector,
    base_proj,
    adapter_down_matrices,
    adapter_up_matrices,
    short_taps,
    medium_taps,
    skip_gain,
    mixer_cot,
    bucket_ids,
):
    rows = token_ids.shape[0]
    vocab, width = embed.shape
    rank = adapter_up_matrices.shape[1]
    span = medium_taps.shape[0]
    wide = 3 * rank
    chunks = width // CHUNK
    fwd, inv1, inv2 = spectrum_tables(rows, span)
    ext = fwd.shape[1]
    out_rows = rows + RIM
    padded = ceil_to(rows + 2 * RIM, 16 * nz)
    ids = jnp.broadcast_to(token_ids[:, None] + 1, (rows, 128))
    vmem = pl.BlockSpec(memory_space=pltpu.VMEM)
    any_space = pl.BlockSpec(memory_space=pl.ANY)
    dma = pltpu.SemaphoreType.DMA
    return pl.pallas_call(
        functools.partial(kernel, ns, nz),
        out_shape=jax.ShapeDtypeStruct((2, BUCKETS, wide), F32),
        in_specs=[vmem, vmem, vmem, any_space, vmem, any_space, vmem, vmem, vmem, any_space]
        + [vmem] * 4,
        out_specs=vmem,
        scratch_shapes=[
            pltpu.VMEM((padded, 128), jnp.int32),
            pltpu.VMEM((padded, vocab), BF),
            pltpu.VMEM((3, rows, width), BF),
            pltpu.VMEM((3, rank, width), BF),
            pltpu.VMEM((rows, width), BF),
            pltpu.VMEM((BUCKETS, width), BF),
            pltpu.VMEM((4, RIM, width), F32),
            pltpu.VMEM((3, RIM, width), F32),
            pltpu.VMEM((4, RIM, width), F32),
            pltpu.VMEM((3, RIM, width), F32),
            pltpu.VMEM((padded, wide + 128), F32),
            pltpu.VMEM((nz - 1, padded // nz, wide + 128), F32),
            pltpu.VMEM((padded, wide), F32),
            pltpu.VMEM((padded, 128), F32),
            pltpu.VMEM((chunks, fwd.shape[0], CHUNK), F32),
            pltpu.VMEM((chunks, ext, CHUNK), F32),
            pltpu.VMEM((chunks, ext, CHUNK), F32),
            pltpu.VMEM((chunks, out_rows, CHUNK), F32),
            pltpu.VMEM((chunks, out_rows, CHUNK), F32),
            pltpu.VMEM((3, rows, rank + BUCKETS), F32),
            pltpu.VMEM((nz, 2 * BUCKETS, wide), F32),
            pltpu.VMEM((ns, 2 * BUCKETS, wide), F32),
            dma((3,)),
            dma((4,)),
            dma((4,)),
            dma((nz - 1,)),
            dma((nz - 1,)),
            dma((2, nz - 1)),
            dma((2, nz - 1)),
            dma((chunks,)),
            dma((chunks,)),
            dma((chunks,)),
            dma((chunks,)),
            dma((nz - 1,)),
            dma((nz - 1,)),
            dma((ns - 1,)),
            dma((ns - 1,)),
        ],
        compiler_params=pltpu.CompilerParams(
            collective_id=0, has_side_effects=True, vmem_limit_bytes=52 * 1024 * 1024
        ),
    )(
        ids,
        embed,
        norm_gain_vector[None],
        base_proj,
        adapter_down_matrices,
        adapter_up_matrices,
        short_taps,
        medium_taps,
        skip_gain[None],
        mixer_cot,
        bucket_ids[None],
        jnp.asarray(fwd, BF),
        jnp.asarray(inv1, BF),
        jnp.asarray(inv2, BF),
    )


def solution(mesh):
    in_specs = (
        P(("parts", "seq")),
        P(None, "tensor"),
        P("tensor"),
        P(None, ("parts", "seq"), "tensor"),
        P("tensor", None),
        P(None, None, "tensor"),
        P(None, None, "tensor"),
        P(None, "tensor"),
        P("tensor"),
        P(("parts", "seq"), "tensor"),
        P("tensor"),
    )
    return jax.shard_map(
        functools.partial(on_device, mesh.shape["seq"], mesh.shape["tensor"]),
        mesh=mesh,
        in_specs=in_specs,
        out_specs=P("parts", None, None),
        check_vma=False,
    )
```

time: 211 us -> 82.8 us (0.39); the launches traced: 207 us -> 82.4 us
  Pallas kernels: 0 us -> 75 us
  blocking collectives: 65.2 us -> 0 us
  waiting for transfers between devices: 35.6 us -> 0 us
  matrix products: 35.3 us -> 0 us
  other arithmetic: 23.9 us -> 0.68 us
  starting transfers between devices: 15.8 us -> 0 us
  between operations: 14.8 us -> 0.03 us
  local copies, waits for them, and re-layouts: 16.5 us -> 6.64 us
    pallas_call x0 -> x1, Pallas kernels: none -> 75 us  [on_device(): pl.pallas_call(functools.partial(kernel, ns, nz), out_shape=jax.ShapeDtyp...]
    psum x1 -> x0, blocking collectives: 65.2 us -> none  [on_device(): raw = lax.psum(raw, ('seq', 'tensor'))]
    psum x1 -> x0, waiting for transfers between devices: 35.6 us -> none  [on_device(): total = lax.psum(jnp.concatenate([piece, squares], axis=1), 'tensor')]
    dot_general x13 -> x0, matrix products: 35.3 us -> none  [the longest x1 18.6 us: on_device(): jnp.einsum('stc,skc->stk', grad_pre, wide, preferred_element_type=F32)]
    ppermute x7 -> x0, starting transfers between devices: 15.8 us -> none  [from_behind(): return lax.ppermute(array, axis, pairs)]
    slice x11 -> x0, local copies, waits for them, and re-layouts: 10.5 us -> none  [the longest x1 2.74 us: on_device(): short_taps[:, j][:, None, :] * streams[:, j:j + rows]]
    convert_element_type x6 -> x0, other arithmetic: 8.92 us -> none  [the longest x1 6.15 us: on_device(): base_proj.astype(F32)]
    add x3 -> x1, other arithmetic: 6.17 us -> 0.68 us  [on_device(): ids = jnp.broadcast_to(token_ids[:, None] + 1, (rows, 128))]
  transfers between devices with their start and end apart: 8 -> 0, of which waited for: 1 -> 0; matrix products, arithmetic and copies ran while one was open for 19% -> 0% of each run, Pallas kernels for 0% -> 0%
where the time goes in v1:
time: 82.8 us; the launch traced here: 82.4 us
  Pallas kernels  75 us (91%)
  local copies, waits for them, and re-layouts  6.64 us (8%)
    pallas_call x1, Pallas kernels, on_device(): pl.pallas_call(functools.partial(kernel, ns, nz), out_shape=jax.ShapeDtyp...  75 us
    unnamed x15, local copies, waits for them, and re-layouts  6.55 us

profile of v1, /device:TPU:0, one launch (start us, length us, event | category | flops | bytes accessed | tf_op | source)
XLA Modules:
  0.0 82.4 jit_solution(10777351338302212502)
XLA Ops:
  0.0 0.7 broadcast_add_fusion
  0.7 0.1 broadcast_in_dim.15.ids_ref
  0.8 0.0 copy-start
  0.8 1.0 %copy-done = bf16[416,400]{1,0:T(8,128)(2,1)S(1)} copy-done((bf16[416,400]{1,0:T(8,128)(2,1)S(1)}, bf16[416,400]{1,0:T(8,128)(2,1)}, u32[]{:S(2)}) %copy-start) | copy-done | bytes 332824
  1.8 0.0 copy-start.1
  1.8 1.0 %copy-done.1 = bf16[272,416]{1,0:T(8,128)(2,1)S(1)} copy-done((bf16[272,416]{1,0:T(8,128)(2,1)S(1)}, bf16[272,416]{1,0:T(8,128)(2,1)}, u32[]{:S(2)}) %copy-start.1) | copy-done | bytes 226328
  2.8 0.0 copy-start.2
  2.8 1.0 %copy-done.2 = bf16[272,416]{1,0:T(8,128)(2,1)S(1)} copy-done((bf16[272,416]{1,0:T(8,128)(2,1)S(1)}, bf16[272,416]{1,0:T(8,128)(2,1)}, u32[]{:S(2)}) %copy-start.2) | copy-done | bytes 226328
  3.7 0.0 copy-start.3
  3.7 0.9 %copy-done.3 = f32[3,7,2048]{2,1,0:T(8,128)S(1)} copy-done((f32[3,7,2048]{2,1,0:T(8,128)S(1)}, f32[3,7,2048]{2,1,0:T(8,128)}, u32[]{:S(2)}) %copy-start.3) | copy-done | bytes 172056
  4.6 0.0 copy-start.4
  4.6 0.7 copy-done.4
  5.3 0.0 copy-start.5
  5.3 0.7 copy-done.5
  6.0 0.0 copy-start.6
  6.0 0.7 copy-done.6
  6.7 75.0 %shard_map.136 = f32[2,16,384]{2,1,0:T(8,128)S(1)} custom-call(s32[256,128]{1,0:T(8,128)S(1)} %broadcast_in_dim.15.ids_ref, bf16[512,2048]{1,0:T(8,128)(2,1)} %embed_ref.1, f32[1,2048]{1,0:T(1,128)S(1)} %bitcast.3, bf16[3,256,2048]{2,1,0:T(8,128)(2,1)} %base_hbm.1, bf16[2048,384]{1,0:T(8,128)(2,1)} %down_ref.1, bf16[3,128,2048]{2,1,0:T(8,128)(2,1)} %up_hbm.1, ...), custom_call_target="tpu_custom_call" | custom-call | tf_op jit(solution)/shard_map/pallas_call | solution.py:498
  81.7 0.6 copy.16
Async XLA Ops:
  0.8 1.0 %copy-start = (bf16[416,400]{1,0:T(8,128)(2,1)S(1)}, bf16[416,400]{1,0:T(8,128)(2,1)}, u32[]{:S(2)}) copy-start(bf16[416,400]{1,0:T(8,128)(2,1)} %constant.8.clone.fwd_ref) | copy-start | bytes 998404
  1.8 1.0 %copy-start.1 = (bf16[272,416]{1,0:T(8,128)(2,1)S(1)}, bf16[272,416]{1,0:T(8,128)(2,1)}, u32[]{:S(2)}) copy-start(bf16[272,416]{1,0:T(8,128)(2,1)} %constant.10.clone.inv2_ref) | copy-start | bytes 678916
  2.8 1.0 %copy-start.2 = (bf16[272,416]{1,0:T(8,128)(2,1)S(1)}, bf16[272,416]{1,0:T(8,128)(2,1)}, u32[]{:S(2)}) copy-start(bf16[272,416]{1,0:T(8,128)(2,1)} %constant.9.clone.inv1_ref) | copy-start | bytes 678916
  3.7 0.9 %copy-start.3 = (f32[3,7,2048]{2,1,0:T(8,128)S(1)}, f32[3,7,2048]{2,1,0:T(8,128)}, u32[]{:S(2)}) copy-start(f32[3,7,2048]{2,1,0:T(8,128)} %short_ref.1) | copy-start | bytes 516100
  4.6 0.7 copy-start.4
  5.3 0.7 copy-start.5
  6.0 0.7 copy-start.6

commit v2 on v1

--- a/solution.py
+++ b/solution.py
@@ -51,35 +51,50 @@
 
 
 def kernel(
+    npart,
     ns,
     nz,
     ids_ref,
-    embed_ref,
+    embed_hbm,
+    gain_hbm,
+    base_hbm,
+    down_hbm,
+    up_hbm,
+    short_hbm,
+    medium_hbm,
+    skip_hbm,
+    cot_hbm,
+    bucket_hbm,
+    fwd_hbm,
+    inv1_hbm,
+    inv2_hbm,
+    out_ref,
+    embed_own,
     gain_ref,
-    base_hbm,
+    base,
     down_ref,
-    up_hbm,
+    up,
     short_ref,
     medium_ref,
     skip_ref,
-    cot_hbm,
+    cot,
     bucket_ref,
     fwd_ref,
     inv1_ref,
     inv2_ref,
-    out_ref,
     ids_ext,
-    one_hot,
-    base,
-    up,
-    cot,
     sketch,
     to_prev,
     to_next,
     from_next,
     from_prev,
     acc,
+    sums,
     rs,
+    tab,
+    ptab,
+    flat,
+    pflat,
     low,
     psk,
     spec,
@@ -87,9 +102,13 @@
     gm,
     fk,
     fv,
+    shift,
     prods,
-    part_z,
-    part_s,
+    part,
+    got_s,
+    got_z,
+    full_sum,
+    done,
     load_sem,
     rim_send,
     rim_recv,
@@ -97,22 +116,27 @@
     rs_recv,
     ag_send,
     ag_recv,
+    pl_send,
+    pl_recv,
+    sib_send,
+    sib_recv,
     kv_send,
     kv_recv,
     gm_send,
     gm_recv,
+    fin_send,
+    fin_recv,
     fz_send,
     fz_recv,
-    fs_send,
-    fs_recv,
 ):
     rows = ids_ref.shape[0]
-    vocab, width = embed_ref.shape
+    vocab, width = embed_hbm.shape
     rank = up_hbm.shape[1]
     span = medium_ref.shape[0]
     taps = short_ref.shape[1]
-    padded = acc.shape[0]
-    own_rows = padded // nz
+    padded = ids_ext.shape[0]
+    words = embed_own.shape[0]
+    own = words // nz
     out_rows = rows + RIM
     all_rows = rows + 2 * RIM
     ext = kv.shape[1]
@@ -121,14 +145,34 @@
     wide = 3 * rank
     s_me = lax.axis_index("seq")
     z_me = lax.axis_index("tensor")
+    p_me = lax.axis_index("parts")
+    core = lax.rem(s_me, 2)
+    sibling = {"seq": s_me + 1 - 2 * core}
     has_prev = s_me > 0
     has_next = s_me < ns - 1
     prev = {"seq": lax.rem(s_me + ns - 1, ns)}
     succ = {"seq": lax.rem(s_me + 1, ns)}
 
+    first_word = pl.multiple_of((p_me * ns + s_me) * words, words)
     loads = [
         pltpu.make_async_copy(src, dst, load_sem.at[i])
-        for i, (src, dst) in enumerate([(base_hbm, base), (up_hbm, up), (cot_hbm, cot)])
+        for i, (src, dst) in enumerate(
+            [
+                (embed_hbm.at[pl.ds(first_word, words)], embed_own),
+                (gain_hbm, gain_ref),
+                (bucket_hbm, bucket_ref),
+                (down_hbm, down_ref),
+                (base_hbm, base),
+                (cot_hbm, cot),
+                (fwd_hbm, fwd_ref),
+                (medium_hbm, medium_ref),
+                (up_hbm, up),
+                (short_hbm, short_ref),
+                (skip_hbm, skip_ref),
+                (inv1_hbm, inv1_ref),
+                (inv2_hbm, inv2_ref),
+            ]
+        )
     ]
     for load in loads:
         load.start()
@@ -142,7 +186,18 @@
         pl.semaphore_signal(
             barrier, inc=1, device_id={"tensor": lax.rem(z_me + d, nz)}, device_id_type=MESH
         )
-    pl.semaphore_wait(barrier, ns + nz - 2)
+    plane = [(dp, ds) for dp in range(npart) for ds in range(0, ns, 2)][1:]
+
+    def plane_peer(dp, ds):
+        return lax.rem(p_me + dp, npart), lax.rem(s_me + ds, ns)
+
+    away = [(dp, ds) for dp, ds in plane if dp > 0]
+    for dp, ds in away:
+        p_to, s_to = plane_peer(dp, ds)
+        pl.semaphore_signal(
+            barrier, inc=1, device_id={"parts": p_to, "seq": s_to}, device_id_type=MESH
+        )
+    pl.semaphore_wait(barrier, ns + nz - 2 + len(away))
 
     def remote(src, dst, send, recv, device):
         return pltpu.make_async_remote_copy(
@@ -197,72 +252,44 @@
     if padded > all_rows:
         ids_ext[all_rows:padded] = jnp.zeros((padded - all_rows, 128), jnp.int32)
     ids_ext[RIM : RIM + rows] = ids_ref[...]
+    for load in loads[:4]:
+        load.wait()
     bucket = bucket_ref[...]
     hit = lax.broadcasted_iota(jnp.int32, (BUCKETS, width), 0) == jnp.bitwise_and(
         bucket, BUCKETS - 1
     )
     sign = jnp.where(bucket >= BUCKETS, -1.0, 1.0).astype(F32)
     sketch[...] = jnp.where(hit, sign, 0.0).astype(BF)
-    acc[...] = jnp.zeros_like(acc)
+    sums[...] = jnp.zeros_like(sums)
     prods[...] = jnp.zeros_like(prods)
-
-    loads[0].wait()
-    loads[2].wait()
-    for s in range(3):
-        to_prev[s] = base[s, 0 : 2 * RIM].astype(F32)[:RIM]
-        to_next[s] = base[s, rows - 2 * RIM : rows].astype(F32)[RIM:]
-    to_prev[3] = cot[0 : 2 * RIM].astype(F32)[:RIM]
-
-    @pl.when(has_next)
-    def _():
-        rim_to_next.start()
-
-    @pl.when(has_prev)
-    def _():
-        rim_to_prev.start()
-
-    @pl.when(has_prev)
-    def _():
-        ids_to_next.wait_recv()
-
-    @pl.when(has_next)
-    def _():
-        ids_to_prev.wait_recv()
-
-    ids = jnp.concatenate([ids_ext[...]] * (vocab // 128), axis=1)
-    one_hot[...] = jnp.where(
-        ids == lax.broadcasted_iota(jnp.int32, (padded, vocab), 1) + 1, 1.0, 0.0
-    ).astype(BF)
 
     def at(k):
         return pl.ds(pl.multiple_of(k * CHUNK, CHUNK), CHUNK)
 
     def front(k, carry):
         cols = at(k)
-        x = nn(one_hot[...], embed_ref[:, cols])
+        x = embed_own[:, cols].astype(F32)
         squares = jnp.sum(x * x, axis=1, keepdims=True)
         gained = x * gain_ref[:, cols]
         high = gained.astype(BF)
         rest = (gained - high.astype(F32)).astype(BF)
         weights = down_ref[cols, :]
-        acc[:, :wide] += nn(high, weights) + nn(rest, weights)
+        sums[:, :wide] += nn(high, weights) + nn(rest, weights)
         table = sketch[:, cols]
-        acc[:, wide : wide + BUCKETS] += nt(high, table) + nt(rest, table)
-        acc[:, wide + BUCKETS : wide + BUCKETS + 1] += squares
+        sums[:, wide : wide + BUCKETS] += nt(high, table) + nt(rest, table)
+        sums[:, wide + BUCKETS : wide + BUCKETS + 1] += squares
         return carry
 
     lax.fori_loop(0, chunks, front, 0)
 
-    def rows_of(z):
-        return pl.ds(pl.multiple_of(z * own_rows, 8), own_rows)
-
-    mine = rows_of(z_me)
+    for z in range(nz):
+        acc[z] = sums[z * own : (z + 1) * own]
     scatters = []
     for d in range(1, nz):
         z_to = lax.rem(z_me + d, nz)
         scatters.append(
             remote(
-                acc.at[rows_of(z_to)],
+                acc.at[z_to],
                 rs.at[d - 1],
                 rs_send.at[d - 1],
                 rs_recv.at[d - 1],
@@ -272,51 +299,123 @@
     for copy in scatters:
         copy.start()
 
-    def filter_spectrum(k, carry):
-        spec[k] = nn(fwd_ref[:, :span], medium_ref[:, at(k)].astype(BF))
-        return carry
-
-    lax.fori_loop(0, chunks, filter_spectrum, 0)
-
-    total = acc[mine, :]
+    loads[4].wait()
+    loads[5].wait()
+    for s in range(3):
+        to_prev[s] = base[s, 0 : 2 * RIM].astype(F32)[:RIM]
+        to_next[s] = base[s, rows - 2 * RIM : rows].astype(F32)[RIM:]
+    to_prev[3] = cot[0 : 2 * RIM].astype(F32)[:RIM]
+
+    @pl.when(has_next)
+    def _():
+        rim_to_next.start()
+
+    @pl.when(has_prev)
+    def _():
+        rim_to_prev.start()
+
+
+    total = acc[z_me]
     for d in range(1, nz):
         scatters[d - 1].wait_recv()
         total = total + rs[d - 1]
     scale = lax.rsqrt(
         total[:, wide + BUCKETS : wide + BUCKETS + 1] / (width * nz) + NORM_EPS
     )
-    low[mine, :] = (total[:, :wide] * (scale * ADAPTER_SCALE)).astype(BF).astype(F32)
-    psk[mine, :] = total[:, wide:] * scale
-    gathers = []
-    for d in range(1, nz):
-        peer = {"tensor": lax.rem(z_me + d, nz)}
-        gathers.append(
-            remote(
-                low.at[mine], low.at[mine], ag_send.at[0, d - 1], ag_recv.at[0, d - 1], peer
+    tab[p_me, s_me, z_me] = (total[:, :wide] * (scale * ADAPTER_SCALE)).astype(BF).astype(F32)
+    ptab[p_me, s_me, z_me] = total[:, wide:] * scale
+
+    def hand_out(which, buffer):
+        lines, planes, siblings = [], [], []
+        block = buffer.at[p_me, s_me, z_me]
+        for d in range(1, nz):
+            lines.append(
+                remote(
+                    block,
+                    block,
+                    ag_send.at[which, d - 1],
+                    ag_recv.at[which, d - 1],
+                    {"tensor": lax.rem(z_me + d, nz)},
+                )
             )
-        )
-    for d in range(1, nz):
-        peer = {"tensor": lax.rem(z_me + d, nz)}
-        gathers.append(
-            remote(
-                psk.at[mine], psk.at[mine], ag_send.at[1, d - 1], ag_recv.at[1, d - 1], peer
+        block = buffer.at[p_me, s_me]
+        for i, (dp, ds) in enumerate(plane):
+            p_to, s_to = plane_peer(dp, ds)
+            planes.append(
+                remote(
+                    block,
+                    block,
+                    pl_send.at[which, i],
+                    pl_recv.at[which, i],
+                    {"parts": p_to, "seq": s_to},
+                )
             )
-        )
-    for copy in gathers:
+        for i, (dp, ds) in enumerate([(0, 0)] + plane):
+            p_of, s_of = lax.rem(p_me + npart - dp, npart), lax.rem(s_me + ns - ds, ns)
+            block = buffer.at[p_of, s_of]
+            siblings.append(
+                remote(block, block, sib_send.at[which, i], sib_recv.at[which, i], sibling)
+            )
+        return lines, planes, siblings
+
+    low_copies = hand_out(0, tab)
+    psk_copies = hand_out(1, ptab)
+    for copy in low_copies[0]:
         copy.start()
-
-    loads[1].wait()
+    for copy in psk_copies[0]:
+        copy.start()
+
+    for load in loads[6:]:
+        load.wait()
+
+    def filter_spectrum(k, carry):
+        spec[k] = nn(fwd_ref[:, :span], medium_ref[:, at(k)].astype(BF))
+        return carry
+
+    for copy in low_copies[0]:
+        copy.wait_recv()
+    for copy in low_copies[1]:
+        copy.start()
+    low_copies[2][0].start()
+
+    lax.fori_loop(0, chunks, filter_spectrum, 0)
 
     @pl.when(has_prev)
     def _():
+        ids_to_next.wait_recv()
         rim_to_next.wait_recv()
 
     @pl.when(has_next)
     def _():
+        ids_to_prev.wait_recv()
         rim_to_prev.wait_recv()
 
-    for copy in gathers[: nz - 1]:
+    ids = jnp.concatenate([ids_ext[...]] * (vocab // 128), axis=1)
+    one_hot = jnp.where(
+        ids == lax.broadcasted_iota(jnp.int32, (padded, vocab), 1) + 1, 1.0, 0.0
+    ).astype(BF)
+
+    for i, copy in enumerate(low_copies[1]):
         copy.wait_recv()
+        low_copies[2][i + 1].start()
+    for copy in psk_copies[0]:
+        copy.wait_recv()
+    for copy in psk_copies[1]:
+        copy.start()
+    psk_copies[2][0].start()
+    for copy in low_copies[2]:
+        copy.wait_recv()
+
+    def flatten(buffer, target):
+        for p in range(npart):
+            for q in range(ns):
+                for z in range(nz):
+                    begin = ((p * ns + q) * nz + z) * own
+                    target[begin : begin + own] = buffer[p, q, z]
+
+    flatten(tab, flat)
+    psk[...] = one_hot
+    low[...] = nn(one_hot, flat[...].astype(BF)).astype(BF)
 
     def kv_copy(k):
         return remote(
@@ -336,14 +435,14 @@
         cols = at(k)
         filtered = []
         for s in range(3):
-            pre = jnp.concatenate(
+            shift[0:all_rows] = jnp.concatenate(
                 [from_prev[s, :, cols], base[s, :, cols].astype(F32), from_next[s, :, cols]],
                 axis=0,
-            ) + nn(low[0:all_rows, s * rank : (s + 1) * rank].astype(BF), up[s, :, cols])
+            ) + nn(low[0:all_rows, s * rank : (s + 1) * rank], up[s, :, cols])
             coeff = short_ref[s, :, cols]
-            running = coeff[0:1] * pre[RIM : RIM + out_rows]
+            running = coeff[0:1] * shift[RIM : RIM + out_rows]
             for j in range(1, taps):
-                running = running + coeff[j : j + 1] * pre[RIM - j : RIM - j + out_rows]
+                running = running + coeff[j : j + 1] * shift[RIM - j : RIM - j + out_rows]
             filtered.append(running)
         fk[k] = filtered[1]
         fv[k] = filtered[2]
@@ -387,60 +486,106 @@
         table = sketch[:, cols]
         for s in range(3):
             if s == 0:
-                stream = cot_ext * mixed
+                shift[0:out_rows] = cot_ext * mixed
             elif s == 1:
-                stream = grad_kv * fv[k]
+                shift[0:out_rows] = grad_kv * fv[k]
             else:
-                stream = grad_kv * fk[k]
+                shift[0:out_rows] = grad_kv * fk[k]
             coeff = short_ref[s, :, cols]
-            running = coeff[0:1] * stream[0:rows]
+            running = coeff[0:1] * shift[0:rows]
             for j in range(1, taps):
-                running = running + coeff[j : j + 1] * stream[j : j + rows]
+                running = running + coeff[j : j + 1] * shift[j : j + rows]
             joined = jnp.concatenate([up[s, :, cols], table], axis=0)
             prods[s] += nt(running.astype(BF), joined)
         return carry
 
     lax.fori_loop(0, chunks, streams_back, 0)
 
-    for copy in gathers[nz - 1 :]:
+    for i, copy in enumerate(psk_copies[1]):
         copy.wait_recv()
-    token_sketch = psk[RIM : RIM + rows, 0:BUCKETS]
+        psk_copies[2][i + 1].start()
+    for copy in psk_copies[2]:
+        copy.wait_recv()
+    flatten(ptab, pflat)
+    words_p = pflat[...]
+    high_p = words_p.astype(BF)
+    rest_p = (words_p - high_p.astype(F32)).astype(BF)
+    picked = psk[...]
+    token_sketch = (nn(picked, high_p) + nn(picked, rest_p))[RIM : RIM + rows, 0:BUCKETS]
     for s in range(3):
         block = slice(s * rank, (s + 1) * rank)
-        part_z[z_me, 0:BUCKETS, block] = ADAPTER_SCALE * tn(token_sketch, prods[s, :, 0:rank])
-        part_z[z_me, BUCKETS : 2 * BUCKETS, block] = tn(
-            prods[s, :, rank:], low[RIM : RIM + rows, block]
-        )
-
-    def share(buffer, me, count, axis, send, recv):
-        copies = [
-            remote(
-                buffer.at[me],
-                buffer.at[me],
-                send.at[d - 1],
-                recv.at[d - 1],
-                {axis: lax.rem(me + d, count)},
-            )
-            for d in range(1, count)
-        ]
+        done[0:BUCKETS, block] = ADAPTER_SCALE * tn(token_sketch, prods[s, :, 0:rank])
+        done[BUCKETS : 2 * BUCKETS, block] = tn(
+            prods[s, :, rank:], low[RIM : RIM + rows, block].astype(F32)
+        )
+
+    few = 2 * BUCKETS // ns
+    for i in range(ns):
+        part[i] = done[i * few : (i + 1) * few]
+    got_s[s_me] = part[s_me]
+    spread = [
+        remote(
+            part.at[lax.rem(s_me + d, ns)],
+            got_s.at[s_me],
+            fin_send.at[0, d - 1],
+            fin_recv.at[0, d - 1],
+            {"seq": lax.rem(s_me + d, ns)},
+        )
+        for d in range(1, ns)
+    ]
+
+    def finish(copies):
         for copy in copies:
             copy.start()
         for copy in copies:
             copy.wait_recv()
+
+    def added(buffer, count):
         total = buffer[0]
         for i in range(1, count):
             total = total + buffer[i]
-        return total, copies
-
-    total, sent_z = share(part_z, z_me, nz, "tensor", fz_send, fz_recv)
-    part_s[s_me] = total
-    raw, sent_s = share(part_s, s_me, ns, "seq", fs_send, fs_recv)
+        return total
+
+    finish(spread)
+    got_z[z_me] = added(got_s, ns)
+    along = [
+        remote(
+            got_z.at[z_me],
+            got_z.at[z_me],
+            fz_send.at[d - 1],
+            fz_recv.at[d - 1],
+            {"tensor": lax.rem(z_me + d, nz)},
+        )
+        for d in range(1, nz)
+    ]
+    finish(along)
+    for copy in spread:
+        copy.wait_send()
+    part[s_me] = added(got_z, nz)
+    back = [
+        remote(
+            part.at[s_me],
+            full_sum.at[s_me],
+            fin_send.at[1, d - 1],
+            fin_recv.at[1, d - 1],
+            {"seq": lax.rem(s_me + d, ns)},
+        )
+        for d in range(1, ns)
+    ]
+    full_sum[s_me] = part[s_me]
+    finish(back)
+    for i in range(ns):
+        done[i * few : (i + 1) * few] = full_sum[i]
+    raw = done[...]
     mean = jnp.sum(raw * raw) / (2 * BUCKETS * wide)
     features = raw * lax.rsqrt(jnp.full((1, wide), FEATURE_EPS, F32) + mean)
     out_ref[0] = features[:BUCKETS]
     out_ref[1] = features[BUCKETS:]
 
-    for copy in scatters + gathers + sent_z + sent_s:
+    pending = scatters + along + back
+    for group in low_copies + psk_copies:
+        pending = pending + group
+    for copy in pending:
         copy.wait_send()
 
     @pl.when(has_next)
@@ -467,6 +612,7 @@
 
 
 def on_device(
+    npart,
     ns,
     nz,
     token_ids,
@@ -490,58 +636,83 @@
     fwd, inv1, inv2 = spectrum_tables(rows, span)
     ext = fwd.shape[1]
     out_rows = rows + RIM
-    padded = ceil_to(rows + 2 * RIM, 16 * nz)
+    padded = ceil_to(rows + 2 * RIM, 16)
+    words = vocab // (npart * ns)
+    own = words // nz
+    peers = npart * ns // 2
+    few = 2 * BUCKETS // ns
     ids = jnp.broadcast_to(token_ids[:, None] + 1, (rows, 128))
     vmem = pl.BlockSpec(memory_space=pltpu.VMEM)
     any_space = pl.BlockSpec(memory_space=pl.ANY)
     dma = pltpu.SemaphoreType.DMA
     return pl.pallas_call(
-        functools.partial(kernel, ns, nz),
+        functools.partial(kernel, npart, ns, nz),
         out_shape=jax.ShapeDtypeStruct((2, BUCKETS, wide), F32),
-        in_specs=[vmem, vmem, vmem, any_space, vmem, any_space, vmem, vmem, vmem, any_space]
-        + [vmem] * 4,
+        in_specs=[vmem] + [any_space] * 13,
         out_specs=vmem,
         scratch_shapes=[
+            pltpu.VMEM((words, width), BF),
+            pltpu.VMEM((1, width), F32),
+            pltpu.VMEM((3, rows, width), BF),
+            pltpu.VMEM((width, wide), BF),
+            pltpu.VMEM((3, rank, width), BF),
+            pltpu.VMEM(short_taps.shape, F32),
+            pltpu.VMEM((span, width), F32),
+            pltpu.VMEM((1, width), F32),
+            pltpu.VMEM((rows, width), BF),
+            pltpu.VMEM((1, width), jnp.int32),
+            pltpu.VMEM(fwd.shape, BF),
+            pltpu.VMEM(inv1.shape, BF),
+            pltpu.VMEM(inv2.shape, BF),
             pltpu.VMEM((padded, 128), jnp.int32),
-            pltpu.VMEM((padded, vocab), BF),
-            pltpu.VMEM((3, rows, width), BF),
-            pltpu.VMEM((3, rank, width), BF),
-            pltpu.VMEM((rows, width), BF),
             pltpu.VMEM((BUCKETS, width), BF),
             pltpu.VMEM((4, RIM, width), F32),
             pltpu.VMEM((3, RIM, width), F32),
             pltpu.VMEM((4, RIM, width), F32),
             pltpu.VMEM((3, RIM, width), F32),
-            pltpu.VMEM((padded, wide + 128), F32),
-            pltpu.VMEM((nz - 1, padded // nz, wide + 128), F32),
-            pltpu.VMEM((padded, wide), F32),
-            pltpu.VMEM((padded, 128), F32),
+            pltpu.VMEM((nz, own, wide + 128), F32),
+            pltpu.VMEM((words, wide + 128), F32),
+            pltpu.VMEM((nz - 1, own, wide + 128), F32),
+            pltpu.VMEM((npart, ns, nz, own, wide), F32),
+            pltpu.VMEM((npart, ns, nz, own, 128), F32),
+            pltpu.VMEM((vocab, wide), F32),
+            pltpu.VMEM((vocab, 128), F32),
+            pltpu.VMEM((padded, wide), BF),
+            pltpu.VMEM((padded, vocab), BF),
             pltpu.VMEM((chunks, fwd.shape[0], CHUNK), F32),
             pltpu.VMEM((chunks, ext, CHUNK), F32),
             pltpu.VMEM((chunks, ext, CHUNK), F32),
             pltpu.VMEM((chunks, out_rows, CHUNK), F32),
             pltpu.VMEM((chunks, out_rows, CHUNK), F32),
+            pltpu.VMEM((padded, CHUNK), F32),
             pltpu.VMEM((3, rows, rank + BUCKETS), F32),
-            pltpu.VMEM((nz, 2 * BUCKETS, wide), F32),
-            pltpu.VMEM((ns, 2 * BUCKETS, wide), F32),
-            dma((3,)),
+            pltpu.VMEM((ns, few, wide), F32),
+            pltpu.VMEM((ns, few, wide), F32),
+            pltpu.VMEM((nz, few, wide), F32),
+            pltpu.VMEM((ns, few, wide), F32),
+            pltpu.VMEM((2 * BUCKETS, wide), F32),
+            dma((13,)),
             dma((4,)),
             dma((4,)),
             dma((nz - 1,)),
             dma((nz - 1,)),
             dma((2, nz - 1)),
             dma((2, nz - 1)),
+            dma((2, peers - 1)),
+            dma((2, peers - 1)),
+            dma((2, peers)),
+            dma((2, peers)),
             dma((chunks,)),
             dma((chunks,)),
             dma((chunks,)),
             dma((chunks,)),
+            dma((2, ns - 1)),
+            dma((2, ns - 1)),
             dma((nz - 1,)),
             dma((nz - 1,)),
-            dma((ns - 1,)),
-            dma((ns - 1,)),
         ],
         compiler_params=pltpu.CompilerParams(
-            collective_id=0, has_side_effects=True, vmem_limit_bytes=52 * 1024 * 1024
+            collective_id=0, has_side_effects=True, vmem_limit_bytes=58 * 1024 * 1024
         ),
     )(
         ids,
@@ -576,7 +747,9 @@
         P("tensor"),
     )
     return jax.shard_map(
-        functools.partial(on_device, mesh.shape["seq"], mesh.shape["tensor"]),
+        functools.partial(
+            on_device, mesh.shape["parts"], mesh.shape["seq"], mesh.shape["tensor"]
+        ),
         mesh=mesh,
         in_specs=in_specs,
         out_specs=P("parts", None, None),

time: 82.8 us -> 63 us (0.76)
  Pallas kernels: 75 us -> 59.9 us
  local copies, waits for them, and re-layouts: 6.64 us -> 2.16 us
    pallas_call x1, Pallas kernels: 75 us -> 59.9 us  [on_device(): pl.pallas_call(functools.partial(kernel, npart, ns, nz), out_shape=jax.Sh...]
    unnamed x15 -> x1, local copies, waits for them, and re-layouts: 6.55 us -> 1.42 us
where the time goes in v2:
time: 63 us; the launch traced here: 62.8 us
  Pallas kernels  59.9 us (95%)
  local copies, waits for them, and re-layouts  2.16 us (3%)
  other arithmetic  0.68 us (1%)
    pallas_call x1, Pallas kernels, on_device(): pl.pallas_call(functools.partial(kernel, npart, ns, nz), out_shape=jax.Sh...  59.9 us
    unnamed x1, local copies, waits for them, and re-layouts  1.42 us

profile of v2, /device:TPU:0, one launch (start us, length us, event | category | flops | bytes accessed | tf_op | source)
XLA Modules:
  0.0 62.8 jit_solution(9844126132288569483)
XLA Ops:
  0.0 0.7 %broadcast_add_fusion = s32[256]{0:T(256)S(1)} fusion(s32[256]{0:T(256)} %param.14), kind=kLoop, calls=%fused_computation | loop fusion | flops 256 | bytes 2048 | tf_op jit(solution)/shard_map/add | solution.py:644
  0.7 0.7 %broadcast_in_dim.15.ids_ref = s32[256,128]{1,0:T(8,128)} broadcast(s32[256]{0:T(256)S(1)} %broadcast_add_fusion), dimensions={0} | broadcast | bytes 132096 | tf_op jit(solution)/shard_map/broadcast_in_dim | solution.py:644
  1.4 59.9 %shard_map.136 = f32[2,16,384]{2,1,0:T(8,128)} custom-call(s32[256,128]{1,0:T(8,128)} %broadcast_in_dim.15.ids_ref, bf16[512,2048]{1,0:T(8,128)(2,1)} %embed_hbm.1, f32[1,2048]{1,0:T(1,128)} %bitcast.3, bf16[3,256,2048]{2,1,0:T(8,128)(2,1)} %base_hbm.1, bf16[2048,384]{1,0:T(8,128)(2,1)} %down_hbm.1, bf16[3,128,2048]{2,1,0:T(8,128)(2,1)} %up_hbm.1, ...), custom_call_target="tpu_custom_call" | custom-call | tf_op jit(solution)/shard_map/pallas_call | solution.py:648
  61.4 1.4 %copy.16 = f32[2,16,384]{2,1,0:T(8,128)} copy(f32[2,16,384]{2,1,0:T(8,128)} %shard_map.136) | data formatting | bytes 98304

commit v3 on v2

--- a/solution.py
+++ b/solution.py
@@ -14,6 +14,7 @@
 ADAPTER_SCALE = 1.5
 RIM = 8
 CHUNK = 256
+BLOCK = 64
 BF = jnp.bfloat16
 F32 = jnp.float32
 HIGHEST = lax.Precision.HIGHEST
@@ -103,6 +104,8 @@
     fk,
     fv,
     shift,
+    spectra,
+    grads,
     prods,
     part,
     got_s,
@@ -261,7 +264,6 @@
     sign = jnp.where(bucket >= BUCKETS, -1.0, 1.0).astype(F32)
     sketch[...] = jnp.where(hit, sign, 0.0).astype(BF)
     sums[...] = jnp.zeros_like(sums)
-    prods[...] = jnp.zeros_like(prods)
 
     def at(k):
         return pl.ds(pl.multiple_of(k * CHUNK, CHUNK), CHUNK)
@@ -417,6 +419,8 @@
     psk[...] = one_hot
     low[...] = nn(one_hot, flat[...].astype(BF)).astype(BF)
 
+    blocks = [(r, BLOCK) for r in range(0, rows, BLOCK)] + [(rows, RIM)]
+
     def kv_copy(k):
         return remote(
             kv.at[k, rows : rows + span], kv.at[k, 0:span], kv_send.at[k], kv_recv.at[k], succ
@@ -433,21 +437,31 @@
 
     def streams_in(k, carry):
         cols = at(k)
-        filtered = []
         for s in range(3):
-            shift[0:all_rows] = jnp.concatenate(
-                [from_prev[s, :, cols], base[s, :, cols].astype(F32), from_next[s, :, cols]],
-                axis=0,
-            ) + nn(low[0:all_rows, s * rank : (s + 1) * rank], up[s, :, cols])
+            mixed_in = nn(low[0:all_rows, s * rank : (s + 1) * rank], up[s, :, cols])
+            shift[0, s, 0:RIM] = from_prev[s, :, cols] + mixed_in[:RIM]
+            for r in range(0, rows, BLOCK):
+                shift[0, s, RIM + r : RIM + r + BLOCK] = (
+                    base[s, r : r + BLOCK, cols].astype(F32) + mixed_in[RIM + r : RIM + r + BLOCK]
+                )
+            shift[0, s, RIM + rows : all_rows] = from_next[s, :, cols] + mixed_in[RIM + rows :]
+
+        def causal(s, r, count):
             coeff = short_ref[s, :, cols]
-            running = coeff[0:1] * shift[RIM : RIM + out_rows]
+            running = coeff[0:1] * shift[0, s, RIM + r : RIM + r + count]
             for j in range(1, taps):
-                running = running + coeff[j : j + 1] * shift[RIM - j : RIM - j + out_rows]
-            filtered.append(running)
-        fk[k] = filtered[1]
-        fv[k] = filtered[2]
-        kv[k, span : span + out_rows] = filtered[1] * filtered[2]
-        gm[k, 0:rows] = cot[:, cols].astype(F32) * filtered[0][0:rows]
+                begin = RIM - j + r
+                running = running + coeff[j : j + 1] * shift[0, s, begin : begin + count]
+            return running
+
+        for r, count in blocks:
+            fk_part = causal(1, r, count)
+            fv_part = causal(2, r, count)
+            fk[k, r : r + count] = fk_part
+            fv[k, r : r + count] = fv_part
+            kv[k, span + r : span + r + count] = fk_part * fv_part
+            if r < rows:
+                gm[k, r : r + count] = cot[r : r + count, cols].astype(F32) * causal(0, r, count)
 
         @pl.when(has_next)
         def _():
@@ -461,45 +475,57 @@
 
     lax.fori_loop(0, chunks, streams_in, 0)
 
-    def streams_back(k, carry):
-        cols = at(k)
-
+    def streams_back(pair, carry):
         @pl.when(has_prev)
         def _():
-            kv_copy(k).wait_recv()
+            for u in range(2):
+                kv_copy(2 * pair + u).wait_recv()
 
         @pl.when(has_next)
         def _():
-            gm_copy(k).wait_recv()
-
-        hr, hi = spec[k, 0:half], spec[k, half:]
-        x = nn(fwd_ref[...], kv[k].astype(BF))
-        xr, xi = x[:half], x[half:]
-        y = jnp.concatenate([xr * hr - xi * hi, xr * hi + xi * hr], axis=0).astype(BF)
-        skip = skip_ref[:, cols]
-        mixed = nn(inv1_ref[...], y)[:out_rows] + skip * kv[k, span : span + out_rows]
-        g = nn(fwd_ref[...], gm[k].astype(BF))
-        gr, gi = g[:half], g[half:]
-        w = jnp.concatenate([gr * hr + gi * hi, gi * hr - gr * hi], axis=0).astype(BF)
-        grad_kv = nn(inv2_ref[...], w)[:out_rows] + skip * gm[k, 0:out_rows]
-        cot_ext = jnp.concatenate([cot[:, cols].astype(F32), from_next[3, :, cols]], axis=0)
-        table = sketch[:, cols]
-        for s in range(3):
-            if s == 0:
-                shift[0:out_rows] = cot_ext * mixed
-            elif s == 1:
-                shift[0:out_rows] = grad_kv * fv[k]
-            else:
-                shift[0:out_rows] = grad_kv * fk[k]
-            coeff = short_ref[s, :, cols]
-            running = coeff[0:1] * shift[0:rows]
-            for j in range(1, taps):
-                running = running + coeff[j : j + 1] * shift[j : j + rows]
-            joined = jnp.concatenate([up[s, :, cols], table], axis=0)
-            prods[s] += nt(running.astype(BF), joined)
+            for u in range(2):
+                gm_copy(2 * pair + u).wait_recv()
+
+        for u in range(2):
+            k = 2 * pair + u
+            cols = at(k)
+            skip = skip_ref[:, cols]
+            x = nn(fwd_ref[...], kv[k].astype(BF))
+            g = nn(fwd_ref[...], gm[k].astype(BF))
+            for r in range(0, half, 16):
+                upper, lower = slice(r, r + 16), slice(half + r, half + r + 16)
+                hr, hi = spec[k, upper], spec[k, lower]
+                xr, xi = x[upper], x[lower]
+                spectra[u, 0, upper] = (xr * hr - xi * hi).astype(BF)
+                spectra[u, 0, lower] = (xr * hi + xi * hr).astype(BF)
+                gr, gi = g[upper], g[lower]
+                spectra[u, 1, upper] = (gr * hr + gi * hi).astype(BF)
+                spectra[u, 1, lower] = (gi * hr - gr * hi).astype(BF)
+            mixed = nn(inv1_ref[...], spectra[u, 0])
+            grad_kv = nn(inv2_ref[...], spectra[u, 1])
+            for r, count in blocks:
+                here = slice(r, r + count)
+                mixed_part = mixed[here] + skip * kv[k, span + r : span + r + count]
+                grad_part = grad_kv[here] + skip * gm[k, here]
+                if r < rows:
+                    cot_part = cot[here, cols].astype(F32)
+                else:
+                    cot_part = from_next[3, :, cols]
+                shift[u, 0, here] = cot_part * mixed_part
+                shift[u, 1, here] = grad_part * fv[k, here]
+                shift[u, 2, here] = grad_part * fk[k, here]
+            for s in range(3):
+                coeff = short_ref[s, :, cols]
+                for r in range(0, rows, BLOCK):
+                    running = coeff[0:1] * shift[u, s, r : r + BLOCK]
+                    for j in range(1, taps):
+                        running = running + coeff[j : j + 1] * shift[u, s, r + j : r + j + BLOCK]
+                    grads[s, r : r + BLOCK, cols] = running.astype(BF)
         return carry
 
-    lax.fori_loop(0, chunks, streams_back, 0)
+    lax.fori_loop(0, chunks // 2, streams_back, 0)
+    for s in range(3):
+        prods[s] = nt(grads[s], jnp.concatenate([up[s], sketch[...]], axis=0))
 
     for i, copy in enumerate(psk_copies[1]):
         copy.wait_recv()
@@ -684,7 +710,9 @@
             pltpu.VMEM((chunks, ext, CHUNK), F32),
             pltpu.VMEM((chunks, out_rows, CHUNK), F32),
             pltpu.VMEM((chunks, out_rows, CHUNK), F32),
-            pltpu.VMEM((padded, CHUNK), F32),
+            pltpu.VMEM((2, 3, padded, CHUNK), F32),
+            pltpu.VMEM((2, 2, fwd.shape[0], CHUNK), BF),
+            pltpu.VMEM((3, rows, width), BF),
             pltpu.VMEM((3, rows, rank + BUCKETS), F32),
             pltpu.VMEM((ns, few, wide), F32),
             pltpu.VMEM((ns, few, wide), F32),

time: 63 us -> 61.6 us (0.978)
  Pallas kernels: 59.9 us -> 58.5 us
    pallas_call x1, Pallas kernels: 59.9 us -> 58.5 us  [on_device(): pl.pallas_call(functools.partial(kernel, npart, ns, nz), out_shape=jax.Sh...]
where the time goes in v3:
time: 61.6 us; the launch traced here: 61.4 us
  Pallas kernels  58.5 us (95%)
  local copies, waits for them, and re-layouts  2.16 us (4%)
  other arithmetic  0.68 us (1%)
    pallas_call x1, Pallas kernels, on_device(): pl.pallas_call(functools.partial(kernel, npart, ns, nz), out_shape=jax.Sh...  58.5 us
    unnamed x1, local copies, waits for them, and re-layouts  1.42 us

profile of v3, /device:TPU:0, one launch (start us, length us, event | category | flops | bytes accessed | tf_op | source)
XLA Modules:
  0.0 61.4 jit_solution(2889984692196068280)
XLA Ops:
  0.0 0.7 %broadcast_add_fusion = s32[256]{0:T(256)S(1)} fusion(s32[256]{0:T(256)} %param.14), kind=kLoop, calls=%fused_computation | loop fusion | flops 256 | bytes 2048 | tf_op jit(solution)/shard_map/add | solution.py:670
  0.7 0.7 %broadcast_in_dim.15.ids_ref = s32[256,128]{1,0:T(8,128)} broadcast(s32[256]{0:T(256)S(1)} %broadcast_add_fusion), dimensions={0} | broadcast | bytes 132096 | tf_op jit(solution)/shard_map/broadcast_in_dim | solution.py:670
  1.4 58.5 %shard_map.136 = f32[2,16,384]{2,1,0:T(8,128)} custom-call(s32[256,128]{1,0:T(8,128)} %broadcast_in_dim.15.ids_ref, bf16[512,2048]{1,0:T(8,128)(2,1)} %embed_hbm.1, f32[1,2048]{1,0:T(1,128)} %bitcast.3, bf16[3,256,2048]{2,1,0:T(8,128)(2,1)} %base_hbm.1, bf16[2048,384]{1,0:T(8,128)(2,1)} %down_hbm.1, bf16[3,128,2048]{2,1,0:T(8,128)(2,1)} %up_hbm.1, ...), custom_call_target="tpu_custom_call" | custom-call | tf_op jit(solution)/shard_map/pallas_call | solution.py:674
  59.9 1.4 %copy.16 = f32[2,16,384]{2,1,0:T(8,128)} copy(f32[2,16,384]{2,1,0:T(8,128)} %shard_map.136) | data formatting | bytes 98304
